TPU v7x, 512 devices: a whole 4x4x16 slice. The times are simulated.
512 devices in a mesh: side: 2 (over core), group: 64 (over y, z), tensor: 4 (over x).
Axes of the slice: x: 4, y: 4, z: 16, core: 2. Of those that a mesh axis runs over, the one named last changes fastest.
Arguments:
- tokens: bfloat16 [2, 2048, 4096], P(None, 'group', ('side', 'tensor'))
- norm_gain: bfloat16 [4096], P(('side', 'tensor')), may hold values from 0.099609375 to 1.8984375
- router_weight: bfloat16 [4096, 64], P(('side', 'tensor')), may hold values from -0.09375 to 0.09375
- expert_ids: int32 [2, 2048, 4], P(None, 'group'), may hold values from 0 to 63, all different within a row; in each aligned block of 32 rows (0 to 31, 32 to 63, ..., all dimensions but the last counted through in order) at most 4 rows name the same one
- w_gate: bfloat16 [64, 4096, 1024], P('group', None, ('side', 'tensor')), may hold values from -0.09375 to 0.09375
- w_up: bfloat16 [64, 4096, 1024], P('group', None, ('side', 'tensor')), may hold values from -0.09375 to 0.09375
- w_down: bfloat16 [64, 1024, 4096], P('group', None, ('side', 'tensor')), may hold values from -0.1875 to 0.1875
Outputs:
- mixed: bfloat16 [2, 2048, 4096], P(None, 'group', ('side', 'tensor'))
Inputs may be any that keep to these rules, and one draw needn't show every extreme that they name: `expert_ids`: each row names 4 different experts. Within each aligned block of 32 rows of a micro-batch no expert is named by more than 4 rows, a bound that some block reaches in every draw.
All inputs are finite; a program needn't handle non-finite values.
Results may differ from a plain program's by a relative error of at most 0.0041.
Values may be sent and summed in bfloat16 or wider, within the bound.
A program may use at most 64 MiB of HBM per device.

v0:
```python
import jax
import jax.numpy as jnp
from jax import lax
from jax.sharding import PartitionSpec as P

D = 4096


def per_device(tokens, norm_gain, router_weight, expert_ids, w_gate, w_up, w_down):
    batches = tokens.shape[0]
    row_count = tokens.shape[1]
    chan_dev = tokens.shape[2]
    experts = router_weight.shape[1]
    picks = expert_ids.shape[2]
    groups = lax.axis_size("group")
    capacity = min(row_count, max(2, 2 * row_count * picks // experts))
    gate_rows = w_gate[0]
    up_rows = w_up[0]
    down_rows = w_down[0]
    results = []
    for which in range(batches):
        prepare_values = tokens[which].astype(jnp.float32)
        scaled = prepare_values * norm_gain.astype(jnp.float32)
        partial_logits = jnp.dot(
            scaled, router_weight.astype(jnp.float32), precision=lax.Precision.HIGHEST
        )
        squares, logit_sums = lax.psum(
            (jnp.sum(prepare_values * prepare_values, axis=1), partial_logits), ("side", "tensor")
        )
        inv_rms = lax.rsqrt(squares / D + 1e-06)[:, None]
        prepare_normed = (scaled * inv_rms).astype(jnp.bfloat16)
        scores = jax.nn.sigmoid(inv_rms * logit_sums)
        chosen = (
            expert_ids[which][:, :, None] == jnp.arange(experts, dtype=jnp.int32)[None, None, :]
        ).astype(jnp.float32)
        picked = jnp.sum(chosen * scores[:, None, :], axis=2)
        gates = 2.5 * picked / jnp.sum(picked, axis=1, keepdims=True)
        flat_choice = chosen.reshape(row_count * picks, experts)
        earlier = jnp.cumsum(flat_choice, axis=0) - flat_choice
        position = (
            jnp.sum(earlier * flat_choice, axis=1).astype(jnp.int32).reshape(row_count, picks)
        )
        target = expert_ids[which] * capacity + position
        place = (
            target[:, :, None] == jnp.arange(experts * capacity, dtype=jnp.int32)[None, None, :]
        ).astype(jnp.float32)
        prepare_placed = jnp.sum(place, axis=1).astype(jnp.bfloat16)
        prepare_weighting = jnp.sum(gates[:, :, None] * place, axis=1)
        prepared = (prepare_values, prepare_normed, prepare_placed, prepare_weighting)
        expand_values, expand_normed, expand_placed, expand_weighting = prepared
        picked_rows = lax.dot_general(
            expand_placed,
            expand_normed,
            (((0,), (0,)), ((), ())),
            preferred_element_type=jnp.float32,
        )
        outgoing = picked_rows.astype(jnp.bfloat16).reshape(
            experts, capacity, expand_normed.shape[1]
        )
        arrived = lax.all_to_all(outgoing, "group", split_axis=0, concat_axis=0, tiled=True)
        portion = lax.all_gather(arrived, ("side", "tensor"), axis=2, tiled=True)
        width_now = portion.shape[2]
        flat_rows = portion.reshape(-1, width_now)
        gate_part = jnp.dot(flat_rows, gate_rows, preferred_element_type=jnp.float32)
        up_part = jnp.dot(flat_rows, up_rows, preferred_element_type=jnp.float32)
        values, normed, placed, weighting = prepared
        expert_out = jnp.dot(
            lax.all_gather(
                (jax.nn.silu(gate_part) * up_part).astype(jnp.bfloat16),
                ("side", "tensor"),
                axis=1,
                tiled=True,
            ),
            down_rows,
            preferred_element_type=jnp.float32,
        )
        expert_out = expert_out.astype(jnp.bfloat16).reshape(groups, capacity, chan_dev)
        returned = lax.all_to_all(
            expert_out, "group", split_axis=0, concat_axis=0, tiled=True
        ).reshape(experts * capacity, chan_dev)
        mixed = values + jnp.dot(
            weighting, returned.astype(jnp.float32), precision=lax.Precision.HIGHEST
        )
        results.append(mixed.astype(jnp.bfloat16))
    return jnp.stack(results)


def solution(mesh):
    placed = (
        P(None, "group", ("side", "tensor")),
        P(("side", "tensor")),
        P(("side", "tensor"), None),
        P(None, "group", None),
        P("group", None, ("side", "tensor")),
        P("group", None, ("side", "tensor")),
        P("group", None, ("side", "tensor")),
    )
    return jax.shard_map(
        per_device,
        mesh=mesh,
        in_specs=placed,
        out_specs=P(None, "group", ("side", "tensor")),
        check_vma=False,
    )
```

profile of v0, /device:TPU:1, one launch (start us, length us, event | category | flops | bytes accessed | tf_op | source)
XLA Modules:
  0.0 223.8 jit_solution(2482318666801734263)
XLA Ops:
  6.5 0.8 convert_element_type.97
  7.3 0.9 fusion.20
  8.2 1.0 fusion.17
  9.2 1.0 fusion.15
  10.3 0.7 slice_bitcast_fusion.1
  12.7 30.4 %all-reduce = (f32[32,64]{1,0:T(8,128)S(1)}, f32[32]{0:T(128)S(1)}, f32[32,64]{1,0:T(8,128)S(1)}, f32[32]{0:T(128)S(1)}) all-reduce(f32[32,64]{1,0:T(8,128)S(1)} %fusion.17, f32[32]{0:T(128)S(1)} %get-tuple-element.6, f32[32,64]{1,0:T(8,128)S(1)} %fusion.15, ...), channel_id=1, replica_groups=mesh['side'=2,'group'=64,'tensor'=4] {'side','tensor'}, use_global_device_ids=true, to_apply=%region_13.14 | all-reduce | flops 4160 | bytes 33280 | tf_op jit(solution)/shard_map/psum | solution.py:27
  43.1 0.7 multiply_add_fusion.1
  44.4 1.0 convolution_convert_fusion
  45.5 35.9 %all_to_all.20 = bf16[64,4,512]{2,1,0:T(4,128)(2,1)} all-to-all(bf16[64,4,512]{2,1,0:T(4,128)(2,1)S(1)} %reshape.111), channel_id=1, replica_groups=mesh['side'=2,'group'=64,'tensor'=4] {'group'}, dimensions={0} | all-to-all | bytes 524288 | tf_op jit(solution)/shard_map/all_to_all | solution.py:60
  82.0 24.7 %all_to_all.21 = bf16[64,4,512]{2,1,0:T(4,128)(2,1)} all-to-all(bf16[64,4,512]{2,1,0:T(4,128)(2,1)S(1)} %reshape.107), channel_id=1, replica_groups=mesh['side'=2,'group'=64,'tensor'=4] {'group'}, dimensions={0} | all-to-all | bytes 524288 | tf_op jit(solution)/shard_map/all_to_all | solution.py:60
  106.7 1.4 all-gather.5.cloned.1.call-done
  108.1 2.5 %reshape.112 = bf16[256,4096]{1,0:T(8,128)(2,1)S(1)} reshape(bf16[64,4,4096]{2,1,0:T(4,128)(2,1)} %all-gather.5.cloned.1.call-done) | data formatting | bytes 4194304 | tf_op jit(solution)/shard_map/reshape | solution.py:63
  110.6 2.0 fusion.10
  112.7 0.7 fusion.1
  113.4 25.4 %all_gather.15 = bf16[256,1024]{1,0:T(8,128)(2,1)S(1)} all-gather(bf16[256,128]{1,0:T(8,128)(2,1)S(1)} %fusion.1), channel_id=1, replica_groups=mesh['side'=2,'group'=64,'tensor'=4] {'side','tensor'}, dimensions={1}, use_global_device_ids=true | all-gather | bytes 589824 | tf_op jit(solution)/shard_map/all_gather | solution.py:68
  139.2 0.8 reshape.113
  140.0 13.4 %all-to-all-start.3 = ((bf16[64,4,512]{2,1,0:T(4,128)(2,1)}), bf16[64,4,512]{2,1,0:T(4,128)(2,1)S(1)}, u32[]{:S(2)}, u32[]{:S(2)}) async-start(bf16[64,4,512]{2,1,0:T(4,128)(2,1)} %reshape.113), calls=%async_computation.3 | async-start | bytes 524288 | tf_op jit(solution)/shard_map/all_to_all | solution.py:78
  153.4 2.5 %reshape.108 = bf16[256,4096]{1,0:T(8,128)(2,1)S(1)} reshape(bf16[64,4,4096]{2,1,0:T(4,128)(2,1)} %all-gather.3.cloned.1.call-done) | data formatting | bytes 4194304 | tf_op jit(solution)/shard_map/reshape | solution.py:63
  155.9 2.0 fusion.12
  158.0 0.7 fusion
  158.7 21.2 %all_gather.13 = bf16[256,1024]{1,0:T(8,128)(2,1)S(1)} all-gather(bf16[256,128]{1,0:T(8,128)(2,1)S(1)} %fusion), channel_id=1, replica_groups=mesh['side'=2,'group'=64,'tensor'=4] {'side','tensor'}, dimensions={1}, use_global_device_ids=true | all-gather | bytes 589824 | tf_op jit(solution)/shard_map/all_gather | solution.py:68
  180.3 0.8 reshape.109
  181.0 14.7 %all-to-all-start.1 = ((bf16[64,4,512]{2,1,0:T(4,128)(2,1)}), bf16[64,4,512]{2,1,0:T(4,128)(2,1)S(1)}, u32[]{:S(2)}, u32[]{:S(2)}) async-start(bf16[64,4,512]{2,1,0:T(4,128)(2,1)} %reshape.109), calls=%async_computation.1 | async-start | bytes 524288 | tf_op jit(solution)/shard_map/all_to_all | solution.py:78
  196.1 20.0 %all-to-all-done.1 = bf16[64,4,512]{2,1,0:T(4,128)(2,1)S(1)} async-done(((bf16[64,4,512]{2,1,0:T(4,128)(2,1)}), bf16[64,4,512]{2,1,0:T(4,128)(2,1)S(1)}, u32[]{:S(2)}, u32[]{:S(2)}) %all-to-all-start.1) | async-done | bytes 262176 | tf_op jit(solution)/shard_map/all_to_all | solution.py:78
  (49 shorter events, 4.9 us)
Async XLA Ops:
  6.5 132.2 %copy-start = (bf16[1,1024,512]{2,1,0:T(8,128)(2,1)S(1)}, bf16[1,1024,512]{2,1,0:T(8,128)(2,1)}, u32[]{:S(2)}) copy-start(bf16[1,1024,512]{2,1,0:T(8,128)(2,1)} %param.13) | copy-start | bytes 3145732
  6.5 75.1 %copy-start.1 = (bf16[2,32,512]{2,1,0:T(8,128)(2,1)S(1)}, bf16[2,32,512]{2,1,0:T(8,128)(2,1)}, u32[]{:S(2)}) copy-start(bf16[2,32,512]{2,1,0:T(8,128)(2,1)} %param.7) | copy-start | bytes 196612
  6.5 101.5 %all-gather.5.cloned.1.call-start = ((), (), s32[]{:S(2)}) async-start(), calls=%async_computation.5 | async-start | bytes 2359296 | tf_op jit(solution)/shard_map/all_gather | solution.py:61
  81.5 71.9 %all-gather.3.cloned.1.call-start = ((), (), s32[]{:S(2)}) async-start(), calls=%async_computation.4 | async-start | bytes 2359296 | tf_op jit(solution)/shard_map/all_gather | solution.py:61
  110.6 2.0 copy-start.2
  140.0 41.1 %all-to-all-start.3 = ((bf16[64,4,512]{2,1,0:T(4,128)(2,1)}), bf16[64,4,512]{2,1,0:T(4,128)(2,1)S(1)}, u32[]{:S(2)}, u32[]{:S(2)}) async-start(bf16[64,4,512]{2,1,0:T(4,128)(2,1)} %reshape.113), calls=%async_computation.3 | async-start | bytes 524288 | tf_op jit(solution)/shard_map/all_to_all | solution.py:78
  155.9 2.0 copy-start.3
  181.0 35.0 %all-to-all-start.1 = ((bf16[64,4,512]{2,1,0:T(4,128)(2,1)}), bf16[64,4,512]{2,1,0:T(4,128)(2,1)S(1)}, u32[]{:S(2)}, u32[]{:S(2)}) async-start(bf16[64,4,512]{2,1,0:T(4,128)(2,1)} %reshape.109), calls=%async_computation.1 | async-start | bytes 524288 | tf_op jit(solution)/shard_map/all_to_all | solution.py:78
Sparse Core Ops, SparseCore 0:
  81.6 26.4 all-gather.4
  110.2 38.4 all-gather.2
where the time goes:
time: 225 us; the launch traced here: 224 us
  blocking collectives  138 us (61%)
  starting transfers between devices  28.1 us (12%)
  waiting for transfers between devices  21.4 us (10%)
  between operations  13.7 us (6%)
  matrix products  10.1 us (4%)
  local copies, waits for them, and re-layouts  8.41 us (4%)
  other arithmetic  4.54 us (2%)
    all_to_all x2, blocking collectives, per_device(): lax.all_to_all(outgoing, 'group', split_axis=0, concat_axis=0, tiled=True)  60.6 us
    all_gather x2, blocking collectives, per_device(): lax.all_gather((jax.nn.silu(gate_part) * up_part).astype(jnp.bfloat16), (...  46.5 us
    psum x1, blocking collectives, per_device(): lax.psum((jnp.sum(prepare_values * prepare_values, axis=1), partial_logit...  30.4 us
    all_to_all x2, starting transfers between devices, per_device(): lax.all_to_all(expert_out, 'group', split_axis=0, concat_axis=0, tiled=True)  28.1 us
    all_to_all x2, waiting for transfers between devices, per_device(): lax.all_to_all(expert_out, 'group', split_axis=0, concat_axis=0, tiled=True)  20 us
    reshape x2, local copies, waits for them, and re-layouts, per_device(): flat_rows = portion.reshape(-1, width_now)  5.09 us
  transfers between devices with their start and end apart: 4, of which 2 were waited for; matrix products, arithmetic and copies ran while one was open for 6% of the time, Pallas kernels for 0%

commit v1 on v0

v1 whole, which is shorter than its diff:
```python
import jax
import jax.numpy as jnp
from jax import lax
from jax.experimental import pallas as pl
from jax.experimental.pallas import tpu as pltpu
from jax.sharding import PartitionSpec as P

MESH = pl.DeviceIdType.MESH
BF = jnp.bfloat16
F32 = jnp.float32
YN, ZN = 4, 16
XN, CN = 4, 2
SLOT = 4
LANES = 128
HALVES = 2


def iota(shape, dim):
    return lax.broadcasted_iota(jnp.int32, shape, dim)


def remote(src, dst, send, recv, peer):
    return pltpu.make_async_remote_copy(
        src_ref=src,
        dst_ref=dst,
        send_sem=send,
        recv_sem=recv,
        device_id=peer,
        device_id_type=MESH,
    )


def kernel(
    tok, gain, router, ids, wg, wu, wd, out,
    wgu, wdv, sel, gates, gx, sb, rb, xb, mt, hb, ob, back,
    wsem, gx_s, gx_r, z_s, z_r, x_s, x_r, m_s, m_r, h_s, h_r, o_s, o_r,
):
    batches, rows, chan = tok.shape
    groups = YN * ZN
    blocks = chan // LANES
    per = blocks * SLOT
    hid = wg.shape[2]
    depth = CN * XN * chan
    span = groups // HALVES
    slots = span * SLOT
    stages = [(m, h * span) for m in range(batches) for h in range(HALVES)]

    g, t, c = (lax.axis_index(a) for a in ("group", "tensor", "side"))
    y, z = lax.div(g, ZN), lax.rem(g, ZN)

    def ahead(d):
        return {"group": lax.rem(y + lax.div(d, ZN), YN) * ZN + lax.rem(z + lax.rem(d, ZN), ZN)}

    def behind(d):
        return {
            "group": lax.rem(y + YN - lax.div(d, ZN), YN) * ZN
            + lax.rem(z + ZN - lax.rem(d, ZN), ZN)
        }

    def near(cs, xr):
        return {"side": lax.rem(c + cs, CN), "tensor": lax.rem(t + xr, XN)}

    right, left, other = near(0, 1), near(0, XN - 1), near(1, 0)
    mates = [(cs, xr) for cs in range(CN) for xr in range(XN) if cs + xr]

    barrier = pltpu.get_barrier_semaphore()

    def greet(i, carry):
        pl.semaphore_signal(barrier, inc=1, device_id=ahead(i + 1), device_id_type=MESH)
        return carry

    lax.fori_loop(0, groups - 1, greet, 0)
    for cs, xr in mates:
        pl.semaphore_signal(barrier, inc=1, device_id=near(cs, xr), device_id_type=MESH)

    for cs in range(CN):
        for xr in range(XN):
            rel = cs * XN + xr
            home = lax.rem(c + cs, CN) * XN + lax.rem(t + xr, XN)
            deep = pl.ds(pl.multiple_of(home * chan, chan), chan)
            pltpu.make_async_copy(wg.at[0, deep, :], wgu.at[rel, :, pl.ds(0, hid)], wsem.at[0]).start()
            pltpu.make_async_copy(wu.at[0, deep, :], wgu.at[rel, :, pl.ds(hid, hid)], wsem.at[0]).start()
            thin = pl.ds(pl.multiple_of(home * hid, hid), hid)
            pltpu.make_async_copy(wd.at[0, thin, :], wdv.at[rel], wsem.at[1]).start()

    tall = blocks * rows
    lane, sub = iota((tall, LANES), 1), iota((tall, LANES), 0)
    earlier = (((sub // rows) == (lane // rows)) & (lane < sub)).astype(BF)
    wide = groups * per
    spread = (iota((LANES, wide), 1) // per == iota((LANES, wide), 0)).astype(BF)
    column, line = iota((tall, wide), 1), iota((tall, wide), 0)
    fits = ((column // SLOT) % blocks) == (line // rows)
    which_slot = (column % SLOT).astype(F32)

    def stacked(m):
        return jnp.concatenate([tok[m, :, b * LANES : (b + 1) * LANES] for b in range(blocks)], axis=0)

    def relative(m):
        named = ids[m]
        rel = (((named // ZN) - y + YN) % YN) * ZN + (((named % ZN) - z + ZN) % ZN)
        return jnp.concatenate([rel] * blocks, axis=0)

    def choose(m):
        rel = relative(m)
        picks = rel.shape[1]
        hit = sum((rel[:, k : k + 1] == lane).astype(F32) for k in range(picks))
        position = jnp.dot(earlier, hit.astype(BF), preferred_element_type=F32)
        code = jnp.where(hit > 0, position, -1.0).astype(BF)
        full = jnp.dot(code, spread, preferred_element_type=F32)
        chosen = jnp.where(fits & (full == which_slot), 1.0, 0.0).astype(BF)
        sel[m] = chosen
        moved = lax.dot_general(
            chosen, stacked(m), (((0,), (0,)), ((), ())), preferred_element_type=F32
        )
        sb[m] = moved.astype(BF).reshape(groups, per, LANES)
        rb[m, 0] = sb[m, 0]

    for m in range(batches):
        choose(m)

    gain_row = gain[...].astype(F32)
    values = tok[...].reshape(batches * rows, chan).astype(F32)
    scaled = values * gain_row
    high = scaled.astype(BF)
    low = (scaled - high.astype(F32)).astype(BF)
    part = jnp.dot(high, router[...], preferred_element_type=F32)
    part = part + jnp.dot(low, router[...], preferred_element_type=F32)
    experts = router.shape[1]
    gx[0, :, 0:experts] = part
    gx[0, :, experts:LANES] = jnp.broadcast_to(
        jnp.sum(values * values, axis=1, keepdims=True), (batches * rows, LANES - experts)
    )

    pl.semaphore_wait(barrier, groups - 1 + len(mates))

    def order(i, lo):
        k, dy = lax.div(i, span // ZN), span // ZN - 1 - lax.rem(i, span // ZN)
        half = lax.div(k + 1, 2)
        dz = lax.rem(ZN // 2 + half - 2 * half * lax.rem(k, 2), ZN)
        return lo + dy * ZN + dz

    def z_out(s):
        m, lo = stages[s]

        def one(i, carry):
            d = order(i, lo)
            remote(sb.at[m, d], rb.at[m, d], z_s.at[s], z_r.at[s], ahead(d)).start()
            return carry

        lax.fori_loop(0, span - (lo == 0), one, 0)

    def z_all(s, src, dst, send, recv):
        m, lo = stages[s]
        first = max(lo, 1)
        some = pl.ds(first, lo + span - first)
        return remote(src.at[m, some], dst.at[m, some], send.at[s], recv.at[s], right)

    def gx_send():
        for cs, xr in mates:
            there = cs * XN + (XN - xr) % XN
            remote(gx.at[0], gx.at[there], gx_s, gx_r, near(cs, xr)).start()

    tile = ZN * per
    i_to, i_from = iota((tile, tile), 0), iota((tile, tile), 1)
    to_b, to_d, to_p = i_to // (ZN * SLOT), (i_to // SLOT) % ZN, i_to % SLOT
    apart = (i_from == to_d * per + to_b * SLOT + to_p).astype(BF)
    from_b, from_d, from_p = i_from // (ZN * SLOT), (i_from // SLOT) % ZN, i_from % SLOT
    together = (i_to == from_d * per + from_b * SLOT + from_p).astype(BF)
    chunk = ZN * SLOT
    diagonal = iota((slots, slots), 0) == iota((slots, slots), 1)

    started = {}

    def x_copy(s, i, src, dst, peer):
        q = remote(src, dst, x_s.at[s, i], x_r.at[s, i], peer)
        q.start()
        started[s, i] = q

    half_rows = slots // 2
    lower, upper = pl.ds(0, half_rows), pl.ds(half_rows, half_rows)

    def arrive(s):
        m, lo = stages[s]
        z_all(s, sb, rb, z_s, z_r).wait_recv()
        squares = []
        for n in range(span // ZN):
            raw = rb[m, lo + n * ZN : lo + (n + 1) * ZN].reshape(tile, LANES)
            moved = jnp.dot(apart, raw, preferred_element_type=F32)
            part = jnp.concatenate([moved[b * chunk : (b + 1) * chunk] for b in range(blocks)], axis=1)
            squares.append(jnp.sum(part * part, axis=1, keepdims=True))
            xb[s, 0, 0, n * chunk : (n + 1) * chunk, :] = (part * gain_row).astype(BF)
        own = xb.at[s, 0, 0]
        x_copy(s, 0, own.at[lower], xb.at[s, 0, XN - 1, lower], right)
        x_copy(s, 1, own.at[upper], xb.at[s, 0, 1, upper], left)
        x_copy(s, 2, own.at[upper], xb.at[s, 0, XN - 1, upper], right)
        x_copy(s, 3, own.at[lower], xb.at[s, 0, 1, lower], left)
        x_copy(s, 4, own, xb.at[s, 1, 0], other)
        square = jnp.concatenate(squares, axis=0)
        flat = jnp.sum(jnp.where(diagonal, square, 0.0), axis=0, keepdims=True)
        mt[s, 0] = jnp.broadcast_to(flat, mt.shape[2:])
        for cs, xr in mates:
            there = cs * XN + (XN - xr) % XN
            remote(mt.at[s, 0], mt.at[s, there], m_s.at[s], m_r.at[s], near(cs, xr)).start()

    def relay(s):
        started[s, 0].wait_recv()
        x_copy(s, 5, xb.at[s, 0, XN - 1, lower], xb.at[s, 0, 2, lower], right)
        started[s, 1].wait_recv()
        x_copy(s, 6, xb.at[s, 0, 1, upper], xb.at[s, 0, 2, upper], left)
        started[s, 2].wait_recv()
        x_copy(s, 7, xb.at[s, 0, XN - 1], xb.at[s, 1, XN - 1], other)
        started[s, 3].wait_recv()
        x_copy(s, 8, xb.at[s, 0, 1], xb.at[s, 1, 1], other)

    def hidden(s):
        started[s, 5].wait_recv()
        started[s, 6].wait_recv()
        x_copy(s, 9, xb.at[s, 0, 2], xb.at[s, 1, 2], other)
        rest = pl.ds(1, CN * XN - 1)
        remote(mt.at[s, rest], mt.at[s, rest], m_s.at[s], m_r.at[s], other).wait_recv()
        total = sum(mt[s, r] for r in range(CN * XN))
        inv = lax.rsqrt(total[0:1] / depth + 1e-06)
        inv = jnp.sum(jnp.where(diagonal, inv, 0.0), axis=1, keepdims=True)
        both = jnp.zeros((slots, 2 * hid), F32)
        for xr in range(XN):
            both = both + jnp.dot(xb[s, 0, xr], wgu[xr], preferred_element_type=F32)
        for i, xr in ((4, 0), (7, XN - 1), (8, 1), (9, 2)):
            started[s, i].wait_recv()
            both = both + jnp.dot(xb[s, 1, xr], wgu[XN + xr], preferred_element_type=F32)
        both = both * inv
        gate, up = both[:, :hid], both[:, hid:]
        hb[s, 0, 0] = (gate / (1.0 + jnp.exp(-gate)) * up).astype(BF)
        for xr in (2, 1, 3):
            q = remote(hb.at[s, 0, 0], hb.at[s, 0, XN - xr], h_s.at[s, xr], h_r.at[s, XN - xr], near(0, xr))
            q.start()
            started[s, "h", xr] = q
        q = remote(hb.at[s, 0, 0], hb.at[s, 1, 0], h_s.at[s, 0], h_r.at[s, 0], other)
        q.start()
        started[s, "h", 0] = q

    def hidden_relay(s):
        for xr in (1, 3, 2):
            remote(hb.at[s, 0, xr], hb.at[s, 0, xr], h_s.at[s, xr], h_r.at[s, xr], other).wait_recv()
            q = remote(hb.at[s, 0, xr], hb.at[s, 1, xr], h_s.at[s, XN + xr], h_r.at[s, XN + xr], other)
            q.start()
            started[s, "h", XN + xr] = q

    def give_back(s):
        m, lo = stages[s]
        done = jnp.zeros((slots, chan), F32)
        for xr in range(XN):
            done = done + jnp.dot(hb[s, 0, xr], wdv[xr], preferred_element_type=F32)
        for xr in (0, 1, 3, 2):
            started[s, "h", XN + xr if xr else 0].wait_recv()
            done = done + jnp.dot(hb[s, 1, xr], wdv[XN + xr], preferred_element_type=F32)
        done = done.astype(BF)
        for n in range(span // ZN):
            part = done[n * chunk : (n + 1) * chunk]
            part = jnp.concatenate([part[:, b * LANES : (b + 1) * LANES] for b in range(blocks)], axis=0)
            moved = jnp.dot(together, part, preferred_element_type=F32).astype(BF)
            ob[m, lo + n * ZN : lo + (n + 1) * ZN] = moved.reshape(ZN, per, LANES)

        def one(i, carry):
            d = order(i, lo)
            remote(ob.at[m, d], back.at[m, d], o_s.at[s], o_r.at[s], behind(d)).start()
            return carry

        lax.fori_loop(0, span - (lo == 0), one, 0)
        if lo == 0:
            back[m, 0] = ob[m, 0]

    def weigh():
        rest = pl.ds(1, CN * XN - 1)
        remote(gx.at[rest], gx.at[rest], gx_s, gx_r, other).wait_recv()
        for m in range(batches):
            total = sum(gx[r, m * rows : (m + 1) * rows] for r in range(CN * XN))
            place = iota((rows, LANES), 1)
            squares = jnp.sum(jnp.where(place == experts, total, 0.0), axis=1, keepdims=True)
            inv = lax.rsqrt(squares / depth + 1e-06)
            scores = 1.0 / (1.0 + jnp.exp(-(inv * total)))
            named = ids[m]
            picked = [
                jnp.sum(jnp.where(named[:, k : k + 1] == place, scores, 0.0), axis=1, keepdims=True)
                for k in range(named.shape[1])
            ]
            whole = sum(picked)
            rel = relative(m)
            weight = jnp.zeros((tall, LANES), F32)
            for k, one in enumerate(picked):
                share = jnp.concatenate([2.5 * one / whole] * blocks, axis=0)
                weight = weight + jnp.where(rel[:, k : k + 1] == lane, share, 0.0)
            high = weight.astype(BF)
            low = (weight - high.astype(F32)).astype(BF)
            for i, some in enumerate((high, low)):
                full = jnp.dot(some, spread, preferred_element_type=F32)
                gates[i, m] = full.astype(BF) * sel[m]

    def combine(m):
        total = stacked(m).astype(F32)
        for s, (which, lo) in enumerate(stages):
            if which == m:
                z_all(s, ob, back, o_s, o_r).wait_recv()
                part = back[m, lo : lo + span].reshape(span * per, LANES)
                for i in range(2):
                    total = total + jnp.dot(
                        gates[i, m, :, lo * per : (lo + span) * per], part, preferred_element_type=F32
                    )
        total = total.astype(out.dtype)
        for b in range(blocks):
            out[m, :, b * LANES : (b + 1) * LANES] = total[b * rows : (b + 1) * rows]

    def weights_ready():
        pltpu.make_async_copy(wgu, wgu, wsem.at[0]).wait()
        pltpu.make_async_copy(wdv, wdv, wsem.at[1]).wait()

    z_out(0)
    z_out(1)
    gx_send()
    z_out(2)
    weights_ready()
    arrive(0)
    z_out(3)
    weigh()
    relay(0)
    arrive(1)
    hidden(0)
    relay(1)
    arrive(2)
    hidden_relay(0)
    hidden(1)
    relay(2)
    give_back(0)
    arrive(3)
    hidden_relay(1)
    hidden(2)
    relay(3)
    give_back(1)
    hidden_relay(2)
    hidden(3)
    give_back(2)
    hidden_relay(3)
    give_back(3)
    for m in range(batches):
        combine(m)

    for q in started.values():
        q.wait_send()
    for s in range(len(stages)):
        z_all(s, sb, rb, z_s, z_r).wait_send()
        z_all(s, ob, back, o_s, o_r).wait_send()
        rest = pl.ds(1, CN * XN - 1)
        remote(mt.at[s, rest], mt.at[s, rest], m_s.at[s], m_r.at[s], other).wait_send()
    rest = pl.ds(1, CN * XN - 1)
    remote(gx.at[rest], gx.at[rest], gx_s, gx_r, other).wait_send()


def per_device(tokens, norm_gain, router_weight, expert_ids, w_gate, w_up, w_down):
    batches, rows, chan = tokens.shape
    groups = YN * ZN
    per = chan // LANES * SLOT
    hid = w_gate.shape[2]
    stages = batches * HALVES
    slots = groups // HALVES * SLOT
    mates = CN * XN
    tall = chan // LANES * rows
    vmem = pl.BlockSpec(memory_space=pltpu.VMEM)
    hbm = pl.BlockSpec(memory_space=pl.ANY)
    dma = pltpu.SemaphoreType.DMA
    blocks = pltpu.VMEM((batches, groups, per, LANES), BF)
    return pl.pallas_call(
        kernel,
        out_shape=jax.ShapeDtypeStruct(tokens.shape, tokens.dtype),
        in_specs=[vmem] * 4 + [hbm] * 3,
        out_specs=vmem,
        scratch_shapes=[
            pltpu.VMEM((mates, chan, 2 * hid), BF),
            pltpu.VMEM((mates, hid, chan), BF),
            pltpu.VMEM((batches, tall, groups * per), BF),
            pltpu.VMEM((2, batches, tall, groups * per), BF),
            pltpu.VMEM((mates, batches * rows, LANES), F32),
            blocks,
            blocks,
            pltpu.VMEM((stages, CN, XN, slots, chan), BF),
            pltpu.VMEM((stages, mates, 8, slots), F32),
            pltpu.VMEM((stages, CN, XN, slots, hid), BF),
            blocks,
            blocks,
            dma((2,)),
            dma,
            dma,
            dma((stages,)),
            dma((stages,)),
            dma((stages, 10)),
            dma((stages, 10)),
            dma((stages,)),
            dma((stages,)),
            dma((stages, mates)),
            dma((stages, mates)),
            dma((stages,)),
            dma((stages,)),
        ],
        compiler_params=pltpu.CompilerParams(
            collective_id=0, has_side_effects=True, vmem_limit_bytes=48 << 20
        ),
        name="routed_experts",
    )(tokens, norm_gain.reshape(1, chan), router_weight, expert_ids, w_gate, w_up, w_down)


def solution(mesh):
    placed = (
        P(None, "group", ("side", "tensor")),
        P(("side", "tensor")),
        P(("side", "tensor"), None),
        P(None, "group", None),
        P("group", None, ("side", "tensor")),
        P("group", None, ("side", "tensor")),
        P("group", None, ("side", "tensor")),
    )
    return jax.shard_map(
        per_device,
        mesh=mesh,
        in_specs=placed,
        out_specs=P(None, "group", ("side", "tensor")),
        check_vma=False,
    )
```

time: 225 us -> 85.3 us (0.38)
  blocking collectives: 138 us -> 0 us
  Pallas kernels: 0 us -> 78.2 us
  starting transfers between devices: 28.1 us -> 0 us
  waiting for transfers between devices: 21.4 us -> 0 us
  between operations: 13.7 us -> 0.04 us
  matrix products: 10.1 us -> 0 us
  other arithmetic: 4.54 us -> 0 us
    pallas_call x0 -> x1, Pallas kernels: none -> 78.2 us  [per_device(): pl.pallas_call(kernel, out_shape=jax.ShapeDtypeStruct(tokens.shape, token...]
    all_to_all x2 -> x0, blocking collectives: 60.6 us -> none  [per_device(): lax.all_to_all(outgoing, 'group', split_axis=0, concat_axis=0, tiled=True)]
    all_gather x2 -> x0, blocking collectives: 46.5 us -> none  [per_device(): lax.all_gather((jax.nn.silu(gate_part) * up_part).astype(jnp.bfloat16), (...]
    psum x1 -> x0, blocking collectives: 30.4 us -> none  [per_device(): lax.psum((jnp.sum(prepare_values * prepare_values, axis=1), partial_logit...]
    all_to_all x2 -> x0, starting transfers between devices: 28.1 us -> none  [per_device(): lax.all_to_all(expert_out, 'group', split_axis=0, concat_axis=0, tiled=True)]
    all_to_all x2 -> x0, waiting for transfers between devices: 20 us -> none  [per_device(): lax.all_to_all(expert_out, 'group', split_axis=0, concat_axis=0, tiled=True)]
    dot_general x12 -> x0, matrix products: 10.1 us -> none  [the longest x2 4.01 us: per_device(): jnp.dot(flat_rows, gate_rows, preferred_element_type=jnp.float32)]
    reshape x8 -> x1, local copies, waits for them, and re-layouts: 6.91 us -> 0.68 us  [per_device(): norm_gain.reshape(1, chan)]
  transfers between devices with their start and end apart: 4 -> 0, of which waited for: 2 -> 0; matrix products, arithmetic and copies ran while one was open for 6% -> 0% of each run, Pallas kernels for 0% -> 0%
where the time goes in v1:
time: 85.3 us; the launch traced here: 85 us
  Pallas kernels  78.2 us (92%)
  local copies, waits for them, and re-layouts  6.75 us (8%)
    pallas_call x1, Pallas kernels, per_device(): pl.pallas_call(kernel, out_shape=jax.ShapeDtypeStruct(tokens.shape, token...  78.2 us
    unnamed x11, local copies, waits for them, and re-layouts  6.07 us

profile of v1, /device:TPU:1, one launch (start us, length us, event | category | flops | bytes accessed | tf_op | source)
XLA Modules:
  0.0 85.0 jit_solution(12340930393207888367)
XLA Ops:
  0.0 0.7 reshape.3.gain
  0.7 0.8 copy.9.ids
  1.5 0.0 copy-start.3
  1.5 1.0 %copy.8.router = bf16[512,64]{1,0:T(8,128)(2,1)S(1)} copy(bf16[512,64]{0,1:T(8,128)(2,1)} %param.9) | data formatting | bytes 131072 | tf_op args[2]
  2.5 0.0 copy-done.3
  2.5 0.0 copy-start
  2.5 1.2 %copy-done = bf16[1,4096,128]{2,1,0:T(8,128)(2,1)S(1)} copy-done((bf16[1,4096,128]{2,1,0:T(8,128)(2,1)S(1)}, bf16[1,4096,128]{2,1,0:T(8,128)(2,1)}, u32[]{:S(2)}) %copy-start) | copy-done | bytes 1048600
  3.7 0.0 copy-start.1
  3.7 1.2 %copy-done.1 = bf16[1,4096,128]{2,1,0:T(8,128)(2,1)S(1)} copy-done((bf16[1,4096,128]{2,1,0:T(8,128)(2,1)S(1)}, bf16[1,4096,128]{2,1,0:T(8,128)(2,1)}, u32[]{:S(2)}) %copy-start.1) | copy-done | bytes 1048600
  4.9 0.0 copy-start.2
  4.9 1.2 %copy-done.2 = bf16[1,1024,512]{2,1,0:T(8,128)(2,1)S(1)} copy-done((bf16[1,1024,512]{2,1,0:T(8,128)(2,1)S(1)}, bf16[1,1024,512]{2,1,0:T(8,128)(2,1)}, u32[]{:S(2)}) %copy-start.2) | copy-done | bytes 1048600
  6.1 78.2 %routed_experts.1 = bf16[2,32,512]{2,1,0:T(8,128)(2,1)S(1)} custom-call(bf16[2,32,512]{2,1,0:T(8,128)(2,1)S(1)} %copy-done.3, bf16[1,512]{1,0:T(2,128)(2,1)S(1)} %reshape.3.gain, bf16[512,64]{1,0:T(8,128)(2,1)S(1)} %copy.8.router, s32[2,32,4]{2,1,0:T(8,128)S(1)} %copy.9.ids, bf16[1,4096,128]{2,1,0:T(8,128)(2,1)S(1)} %copy-done, ...), custom_call_target="tpu_custom_call" | custom-call | tf_op jit(solution)/shard_map/routed_experts/pallas_call | solution.py:370
  84.3 0.6 copy.11
Async XLA Ops:
  1.5 1.0 %copy-start.3 = (bf16[2,32,512]{2,1,0:T(8,128)(2,1)S(1)}, bf16[2,32,512]{2,1,0:T(8,128)(2,1)}, u32[]{:S(2)}) copy-start(bf16[2,32,512]{2,1,0:T(8,128)(2,1)} %tok.1) | copy-start | bytes 196612
  2.5 1.2 %copy-start = (bf16[1,4096,128]{2,1,0:T(8,128)(2,1)S(1)}, bf16[1,4096,128]{2,1,0:T(8,128)(2,1)}, u32[]{:S(2)}) copy-start(bf16[1,4096,128]{2,1,0:T(8,128)(2,1)} %wg.1) | copy-start | bytes 3145732
  3.7 1.2 %copy-start.1 = (bf16[1,4096,128]{2,1,0:T(8,128)(2,1)S(1)}, bf16[1,4096,128]{2,1,0:T(8,128)(2,1)}, u32[]{:S(2)}) copy-start(bf16[1,4096,128]{2,1,0:T(8,128)(2,1)} %wu.1) | copy-start | bytes 3145732
  4.9 1.2 %copy-start.2 = (bf16[1,1024,512]{2,1,0:T(8,128)(2,1)S(1)}, bf16[1,1024,512]{2,1,0:T(8,128)(2,1)}, u32[]{:S(2)}) copy-start(bf16[1,1024,512]{2,1,0:T(8,128)(2,1)} %wd.1) | copy-start | bytes 3145732

commit v2 on v1

v2 whole, which is shorter than its diff:
```python
import jax
import jax.numpy as jnp
from jax import lax
from jax.experimental import pallas as pl
from jax.experimental.pallas import tpu as pltpu
from jax.sharding import PartitionSpec as P

MESH = pl.DeviceIdType.MESH
BF = jnp.bfloat16
F32 = jnp.float32
YN, ZN = 4, 16
XN, CN = 4, 2
SLOT = 4
LANES = 128


def iota(shape, dim):
    return lax.broadcasted_iota(jnp.int32, shape, dim)


def remote(src, dst, send, recv, peer):
    return pltpu.make_async_remote_copy(
        src_ref=src,
        dst_ref=dst,
        send_sem=send,
        recv_sem=recv,
        device_id=peer,
        device_id_type=MESH,
    )


def kernel(
    tok_in, gain, router_in, ids_in, wg, wu, wd, out,
    tok, router, ids, wgu, wdv, sel, gates, gx, sb, rb, xb, mt, hb, ob, back,
    wsem, gx_s, gx_r, z_s, z_r, x_s, x_r, m_s, m_r, h_s, h_r, o_s, o_r,
):
    batches, rows, chan = tok.shape
    groups = YN * ZN
    blocks = chan // LANES
    per = blocks * SLOT
    hid = wg.shape[2]
    depth = CN * XN * chan
    slots = ZN * batches * SLOT
    step = ZN // batches

    g, t, c = (lax.axis_index(a) for a in ("group", "tensor", "side"))
    y, z = lax.div(g, ZN), lax.rem(g, ZN)

    y_at = [lax.rem(y + i, YN) * ZN for i in range(YN)]
    z_at = [lax.rem(z + i, ZN) for i in range(ZN)]

    def ahead(d):
        return {"group": y_at[d // ZN] + z_at[d % ZN]}

    def behind(d):
        return {"group": y_at[-(d // ZN) % YN] + z_at[-(d % ZN) % ZN]}

    def near(cs, xr):
        return {"side": lax.rem(c + cs, CN), "tensor": lax.rem(t + xr, XN)}

    right, left, other = near(0, 1), near(0, XN - 1), near(1, 0)
    mates = [(cs, xr) for cs in range(CN) for xr in range(XN) if cs + xr]

    sent, coming = [], {}

    def launch(key, q):
        q.start()
        sent.append(q)
        coming[key] = q

    def receive(*key):
        coming.pop(key).wait_recv()

    barrier = pltpu.get_barrier_semaphore()

    for d in sorted(range(1, groups), key=lambda d: -min(d % ZN, ZN - d % ZN)):
        pl.semaphore_signal(barrier, inc=1, device_id=ahead(d), device_id_type=MESH)
    for cs, xr in mates:
        pl.semaphore_signal(barrier, inc=1, device_id=near(cs, xr), device_id_type=MESH)

    copies = [
        pltpu.make_async_copy(src, dst, wsem.at[2 + i])
        for i, (src, dst) in enumerate(((ids_in, ids), (tok_in, tok), (router_in, router)))
    ]
    for q in copies:
        q.start()

    for cs in range(CN):
        for xr in range(XN):
            rel = cs * XN + xr
            home = lax.rem(c + cs, CN) * XN + lax.rem(t + xr, XN)
            deep = pl.ds(pl.multiple_of(home * chan, chan), chan)
            pltpu.make_async_copy(wg.at[0, deep, :], wgu.at[rel, :, pl.ds(0, hid)], wsem.at[0]).start()
            pltpu.make_async_copy(wu.at[0, deep, :], wgu.at[rel, :, pl.ds(hid, hid)], wsem.at[0]).start()
            thin = pl.ds(pl.multiple_of(home * hid, hid), hid)
            pltpu.make_async_copy(wd.at[0, thin, :], wdv.at[rel], wsem.at[1]).start()

    tall = blocks * rows
    lane, sub = iota((tall, LANES), 1), iota((tall, LANES), 0)
    earlier = (((sub // rows) == (lane // rows)) & (lane < sub)).astype(BF)
    wide = groups * per
    spread = (iota((LANES, wide), 1) // per == iota((LANES, wide), 0)).astype(BF)
    column, line = iota((tall, wide), 1), iota((tall, wide), 0)
    fits = ((column // SLOT) % blocks) == (line // rows)
    which_slot = (column % SLOT).astype(F32)

    def stacked(m):
        return jnp.concatenate([tok[m, :, b * LANES : (b + 1) * LANES] for b in range(blocks)], axis=0)

    upright = iota((rows, rows), 0) == iota((rows, rows), 1)

    def columns(flat):
        zero = jnp.zeros((), flat.dtype)
        return [
            jnp.sum(jnp.where(upright, flat[k : k + 1], zero), axis=1, keepdims=True)
            for k in range(flat.shape[0])
        ]

    def relative(m):
        found = []
        for named in columns(ids[m]):
            rel = (((named // ZN) - y + YN) % YN) * ZN + (((named % ZN) - z + ZN) % ZN)
            found.append(jnp.concatenate([rel] * blocks, axis=0))
        return found

    def choose(m):
        hit = sum((rel == lane).astype(F32) for rel in relative(m))
        position = jnp.dot(earlier, hit.astype(BF), preferred_element_type=F32)
        code = jnp.where(hit > 0, position, -1.0).astype(BF)
        full = jnp.dot(code, spread, preferred_element_type=F32)
        chosen = jnp.where(fits & (full == which_slot), 1.0, 0.0).astype(BF)
        sel[m] = chosen
        moved = lax.dot_general(
            chosen, stacked(m), (((0,), (0,)), ((), ())), preferred_element_type=F32
        )
        sb[:, m * per : (m + 1) * per, :] = moved.astype(BF).reshape(groups, per, LANES)

    for q in copies[:2]:
        q.wait()
    for m in range(batches):
        choose(m)
    rb[0] = sb[0]

    gain_row = gain[...].astype(F32).reshape(1, chan)
    values = tok[...].reshape(batches * rows, chan).astype(F32)
    scaled = values * gain_row
    high = scaled.astype(BF)
    low = (scaled - high.astype(F32)).astype(BF)
    copies[2].wait()
    across = (((1,), (1,)), ((), ()))
    part = lax.dot_general(high, router[...], across, preferred_element_type=F32)
    part = part + lax.dot_general(low, router[...], across, preferred_element_type=F32)
    squares = jnp.sum(values * values, axis=1, keepdims=True)
    place_of = iota((rows, router.shape[0]), 1)

    def flatten(column):
        return jnp.sum(jnp.where(upright, column, 0.0), axis=0, keepdims=True)

    gx[0] = jnp.zeros(gx.shape[1:], F32)
    for m in range(batches):
        these = slice(m * rows, (m + 1) * rows)
        named = columns(ids[m])
        for k, one in enumerate(named):
            mine = jnp.sum(jnp.where(one == place_of, part[these], 0.0), axis=1, keepdims=True)
            gx[0, m, k : k + 1, :] = flatten(mine)
        gx[0, m, len(named) : len(named) + 1, :] = flatten(squares[these])

    pl.semaphore_wait(barrier, groups - 1 + len(mates))

    def far_first(s):
        return sorted(range(max(s * ZN, 1), (s + 1) * ZN), key=lambda d: -min(d % ZN, ZN - d % ZN))

    def whole(s, src, dst, send, recv):
        some = pl.ds(max(s * ZN, 1), ZN - (s == 0))
        q = remote(src.at[some], dst.at[some], send.at[s], recv.at[s], right)
        sent.append(q)
        return q

    def z_out(s):
        for d in far_first(s):
            remote(sb.at[d], rb.at[d], z_s.at[s], z_r.at[s], ahead(d)).start()
        coming["z", s] = whole(s, sb, rb, z_s, z_r)

    def gx_send():
        for cs, xr in mates:
            there = cs * XN + (XN - xr) % XN
            remote(gx.at[0], gx.at[there], gx_s, gx_r, near(cs, xr)).start()
        rest = pl.ds(1, CN * XN - 1)
        q = remote(gx.at[rest], gx.at[rest], gx_s, gx_r, other)
        sent.append(q)
        coming["g",] = q

    tile = ZN * per
    i_to, i_from = iota((tile, tile), 0), iota((tile, tile), 1)
    to_b, to_d, to_p = i_to // (ZN * SLOT), (i_to // SLOT) % ZN, i_to % SLOT
    apart = (i_from == to_d * per + to_b * SLOT + to_p).astype(BF)
    from_b, from_d, from_p = i_from // (ZN * SLOT), (i_from // SLOT) % ZN, i_from % SLOT
    together = (i_to == from_d * per + from_b * SLOT + from_p).astype(BF)
    chunk = ZN * SLOT
    diagonal = iota((slots, slots), 0) == iota((slots, slots), 1)

    def x_copy(s, i, src, dst, peer):
        launch(("x", s, i), remote(src, dst, x_s.at[s, i], x_r.at[s, i], peer))

    lower, upper = pl.ds(0, slots // 2), pl.ds(slots // 2, slots // 2)

    def arrive(s):
        receive("z", s)
        squares = []
        for n in range(batches):
            raw = rb[s * ZN + n * step : s * ZN + (n + 1) * step].reshape(tile, LANES)
            moved = jnp.dot(apart, raw, preferred_element_type=F32)
            part = jnp.concatenate([moved[b * chunk : (b + 1) * chunk] for b in range(blocks)], axis=1)
            squares.append(jnp.sum(part * part, axis=1, keepdims=True))
            xb[s, 0, 0, n * chunk : (n + 1) * chunk, :] = (part * gain_row).astype(BF)
        own = xb.at[s, 0, 0]
        x_copy(s, 0, own.at[lower], xb.at[s, 0, XN - 1, lower], right)
        x_copy(s, 1, own.at[upper], xb.at[s, 0, 1, upper], left)
        x_copy(s, 2, own.at[upper], xb.at[s, 0, XN - 1, upper], right)
        x_copy(s, 3, own.at[lower], xb.at[s, 0, 1, lower], left)
        x_copy(s, 4, own, xb.at[s, 1, 0], other)
        square = jnp.concatenate(squares, axis=0)
        flat = jnp.sum(jnp.where(diagonal, square, 0.0), axis=0, keepdims=True)
        mt[s, 0] = jnp.broadcast_to(flat, mt.shape[2:])
        for cs, xr in mates:
            there = cs * XN + (XN - xr) % XN
            remote(mt.at[s, 0], mt.at[s, there], m_s.at[s], m_r.at[s], near(cs, xr)).start()
        rest = pl.ds(1, CN * XN - 1)
        q = remote(mt.at[s, rest], mt.at[s, rest], m_s.at[s], m_r.at[s], other)
        sent.append(q)
        coming["m", s] = q

    def relay(s):
        receive("x", s, 0)
        x_copy(s, 5, xb.at[s, 0, XN - 1, lower], xb.at[s, 0, 2, lower], right)
        receive("x", s, 1)
        x_copy(s, 6, xb.at[s, 0, 1, upper], xb.at[s, 0, 2, upper], left)
        receive("x", s, 2)
        x_copy(s, 7, xb.at[s, 0, XN - 1], xb.at[s, 1, XN - 1], other)
        receive("x", s, 3)
        x_copy(s, 8, xb.at[s, 0, 1], xb.at[s, 1, 1], other)

    def hidden(s):
        receive("x", s, 5)
        receive("x", s, 6)
        x_copy(s, 9, xb.at[s, 0, 2], xb.at[s, 1, 2], other)
        acts = jnp.zeros((slots, 2 * hid), F32)
        for xr in range(XN):
            acts = acts + jnp.dot(xb[s, 0, xr], wgu[xr], preferred_element_type=F32)
        receive("m", s)
        total = sum(mt[s, r] for r in range(CN * XN))
        inv = lax.rsqrt(total[0:1] / depth + 1e-06)
        inv = jnp.sum(jnp.where(diagonal, inv, 0.0), axis=1, keepdims=True)
        for i, xr in ((4, 0), (7, XN - 1), (8, 1), (9, 2)):
            receive("x", s, i)
            acts = acts + jnp.dot(xb[s, 1, xr], wgu[XN + xr], preferred_element_type=F32)
        acts = acts * inv
        gate, up = acts[:, :hid], acts[:, hid:]
        hb[s, 0, 0] = (gate / (1.0 + jnp.exp(-gate)) * up).astype(BF)
        for xr in (2, 1, 3):
            there = hb.at[s, 0, XN - xr]
            launch(("h", s, 0, XN - xr), remote(hb.at[s, 0, 0], there, h_s.at[s, xr], h_r.at[s, XN - xr], near(0, xr)))
        launch(("h", s, 1, 0), remote(hb.at[s, 0, 0], hb.at[s, 1, 0], h_s.at[s, 0], h_r.at[s, 0], other))

    def hidden_relay(s):
        for xr in (1, 3, 2):
            receive("h", s, 0, xr)
            there = hb.at[s, 1, xr]
            launch(("h", s, 1, xr), remote(hb.at[s, 0, xr], there, h_s.at[s, XN + xr], h_r.at[s, XN + xr], other))

    def give_back(s):
        done = jnp.zeros((slots, chan), F32)
        for xr in range(XN):
            done = done + jnp.dot(hb[s, 0, xr], wdv[xr], preferred_element_type=F32)
        for xr in (0, 1, 3, 2):
            receive("h", s, 1, xr)
            done = done + jnp.dot(hb[s, 1, xr], wdv[XN + xr], preferred_element_type=F32)
        done = done.astype(BF)
        for n in range(batches):
            part = done[n * chunk : (n + 1) * chunk]
            part = jnp.concatenate([part[:, b * LANES : (b + 1) * LANES] for b in range(blocks)], axis=0)
            moved = jnp.dot(together, part, preferred_element_type=F32).astype(BF)
            ob[s * ZN + n * step : s * ZN + (n + 1) * step] = moved.reshape(step, batches * per, LANES)
        for d in far_first(s):
            remote(ob.at[d], back.at[d], o_s.at[s], o_r.at[s], behind(d)).start()
        if s == 0:
            back[0] = ob[0]
        coming["o", s] = whole(s, ob, back, o_s, o_r)

    def weigh():
        receive("g")
        for m in range(batches):
            picks = ids.shape[1]
            total = sum(gx[r, m] for r in range(CN * XN))
            inv = lax.rsqrt(total[picks : picks + 1] / depth + 1e-06)
            scores = 1.0 / (1.0 + jnp.exp(-(inv * total[0:picks])))
            shares = 2.5 * scores / jnp.sum(scores, axis=0, keepdims=True)
            weight = jnp.zeros((tall, LANES), F32)
            for rel, share in zip(relative(m), columns(shares), strict=True):
                weight = weight + jnp.where(rel == lane, jnp.concatenate([share] * blocks, axis=0), 0.0)
            high = weight.astype(BF)
            low = (weight - high.astype(F32)).astype(BF)
            for i, some in enumerate((high, low)):
                full = jnp.dot(some, spread, preferred_element_type=F32)
                gates[i, m] = full.astype(BF) * sel[m]

    def combine():
        totals = [stacked(m).astype(F32) for m in range(batches)]
        for s in range(YN):
            receive("o", s)
            for m in range(batches):
                part = back[s * ZN : (s + 1) * ZN, m * per : (m + 1) * per, :].reshape(ZN * per, LANES)
                for i in range(2):
                    some = gates[i, m, :, s * ZN * per : (s + 1) * ZN * per]
                    totals[m] = totals[m] + jnp.dot(some, part, preferred_element_type=F32)
        for m, total in enumerate(totals):
            total = total.astype(out.dtype)
            for b in range(blocks):
                out[m, :, b * LANES : (b + 1) * LANES] = total[b * rows : (b + 1) * rows]

    def weights_ready():
        pltpu.make_async_copy(wgu, wgu, wsem.at[0]).wait()
        pltpu.make_async_copy(wdv, wdv, wsem.at[1]).wait()

    for s in range(YN):
        z_out(s)
    gx_send()
    weights_ready()
    arrive(0)
    relay(0)
    arrive(1)
    hidden(0)
    relay(1)
    weigh()
    arrive(2)
    hidden_relay(0)
    hidden(1)
    relay(2)
    give_back(0)
    arrive(3)
    hidden_relay(1)
    hidden(2)
    relay(3)
    give_back(1)
    hidden_relay(2)
    hidden(3)
    give_back(2)
    hidden_relay(3)
    give_back(3)
    combine()

    for q in sent:
        q.wait_send()


def per_device(tokens, norm_gain, router_weight, expert_ids, w_gate, w_up, w_down):
    batches, rows, chan = tokens.shape
    groups = YN * ZN
    per = chan // LANES * SLOT
    hid = w_gate.shape[2]
    stages = YN
    slots = ZN * batches * SLOT
    mates = CN * XN
    tall = chan // LANES * rows
    vmem = pl.BlockSpec(memory_space=pltpu.VMEM)
    hbm = pl.BlockSpec(memory_space=pltpu.HBM)
    dma = pltpu.SemaphoreType.DMA
    blocks = pltpu.VMEM((groups, batches * per, LANES), BF)
    return pl.pallas_call(
        kernel,
        out_shape=jax.ShapeDtypeStruct(tokens.shape, tokens.dtype),
        in_specs=[hbm, vmem] + [hbm] * 5,
        out_specs=vmem,
        scratch_shapes=[
            pltpu.VMEM(tokens.shape, tokens.dtype),
            pltpu.VMEM(router_weight.shape[::-1], router_weight.dtype),
            pltpu.VMEM((batches, expert_ids.shape[2], rows), expert_ids.dtype),
            pltpu.VMEM((mates, chan, 2 * hid), BF),
            pltpu.VMEM((mates, hid, chan), BF),
            pltpu.VMEM((batches, tall, groups * per), BF),
            pltpu.VMEM((2, batches, tall, groups * per), BF),
            pltpu.VMEM((mates, batches, 8, rows), F32),
            blocks,
            blocks,
            pltpu.VMEM((stages, CN, XN, slots, chan), BF),
            pltpu.VMEM((stages, mates, 8, slots), F32),
            pltpu.VMEM((stages, CN, XN, slots, hid), BF),
            blocks,
            blocks,
            dma((5,)),
            dma,
            dma,
            dma((stages,)),
            dma((stages,)),
            dma((stages, 10)),
            dma((stages, 10)),
            dma((stages,)),
            dma((stages,)),
            dma((stages, mates)),
            dma((stages, mates)),
            dma((stages,)),
            dma((stages,)),
        ],
        compiler_params=pltpu.CompilerParams(
            collective_id=0, has_side_effects=True, vmem_limit_bytes=(64 << 20) - (128 << 10)
        ),
        name="routed_experts",
    )(
        tokens,
        norm_gain,
        router_weight.T,
        expert_ids.transpose(0, 2, 1),
        w_gate,
        w_up,
        w_down,
    )


def solution(mesh):
    placed = (
        P(None, "group", ("side", "tensor")),
        P(("side", "tensor")),
        P(("side", "tensor"), None),
        P(None, "group", None),
        P("group", None, ("side", "tensor")),
        P("group", None, ("side", "tensor")),
        P("group", None, ("side", "tensor")),
    )
    return jax.shard_map(
        per_device,
        mesh=mesh,
        in_specs=placed,
        out_specs=P(None, "group", ("side", "tensor")),
        check_vma=False,
    )
```

time: 85.3 us -> 79.4 us (0.931)
  local copies, waits for them, and re-layouts: 6.75 us -> 1.47 us
    unnamed x11 -> x1, local copies, waits for them, and re-layouts: 6.07 us -> 1.47 us
where the time goes in v2:
time: 79.4 us; the launch traced here: 79.2 us
  Pallas kernels  77.7 us (98%)
  local copies, waits for them, and re-layouts  1.47 us (2%)
    pallas_call x1, Pallas kernels, per_device(): pl.pallas_call(kernel, out_shape=jax.ShapeDtypeStruct(tokens.shape, token...  77.7 us

profile of v2, /device:TPU:1, one launch (start us, length us, event | category | flops | bytes accessed | tf_op | source)
XLA Modules:
  0.0 79.2 jit_solution(9548824009344716715)
XLA Ops:
  0.0 77.7 %routed_experts.1 = bf16[2,32,512]{2,1,0:T(8,128)(2,1)} custom-call(bf16[2,32,512]{2,1,0:T(8,128)(2,1)} %tok_in.1, bf16[512]{0:T(512)(128)(2,1)} %gain.1, bf16[64,512]{1,0:T(8,128)(2,1)} %bitcast.2, s32[2,4,32]{2,1,0:T(4,128)} %bitcast.3, bf16[1,4096,128]{2,1,0:T(8,128)(2,1)} %wg.1, bf16[1,4096,128]{2,1,0:T(8,128)(2,1)} %wu.1, bf16[1,1024,512]{2,1,0:T(8,128)(2,1)} %wd.1), custom_call_target="tpu_custom_call" | custom-call | tf_op jit(solution)/shard_map/routed_experts/pallas_call | solution.py:369
  77.7 1.5 %copy.9 = bf16[2,32,512]{2,1,0:T(8,128)(2,1)} copy(bf16[2,32,512]{2,1,0:T(8,128)(2,1)} %routed_experts.1) | data formatting | bytes 131072

commit v3 on v2

--- a/solution.py
+++ b/solution.py
@@ -165,6 +165,15 @@
             gx[0, m, k : k + 1, :] = flatten(mine)
         gx[0, m, len(named) : len(named) + 1, :] = flatten(squares[these])
 
+    tile = ZN * per
+    i_to, i_from = iota((tile, tile), 0), iota((tile, tile), 1)
+    to_b, to_d, to_p = i_to // (ZN * SLOT), (i_to // SLOT) % ZN, i_to % SLOT
+    apart = (i_from == to_d * per + to_b * SLOT + to_p).astype(BF)
+    from_b, from_d, from_p = i_from // (ZN * SLOT), (i_from // SLOT) % ZN, i_from % SLOT
+    together = (i_to == from_d * per + from_b * SLOT + from_p).astype(BF)
+    chunk = ZN * SLOT
+    diagonal = iota((slots, slots), 0) == iota((slots, slots), 1)
+
     pl.semaphore_wait(barrier, groups - 1 + len(mates))
 
     def far_first(s):
@@ -189,15 +198,6 @@
         q = remote(gx.at[rest], gx.at[rest], gx_s, gx_r, other)
         sent.append(q)
         coming["g",] = q
-
-    tile = ZN * per
-    i_to, i_from = iota((tile, tile), 0), iota((tile, tile), 1)
-    to_b, to_d, to_p = i_to // (ZN * SLOT), (i_to // SLOT) % ZN, i_to % SLOT
-    apart = (i_from == to_d * per + to_b * SLOT + to_p).astype(BF)
-    from_b, from_d, from_p = i_from // (ZN * SLOT), (i_from // SLOT) % ZN, i_from % SLOT
-    together = (i_to == from_d * per + from_b * SLOT + from_p).astype(BF)
-    chunk = ZN * SLOT
-    diagonal = iota((slots, slots), 0) == iota((slots, slots), 1)
 
     def x_copy(s, i, src, dst, peer):
         launch(("x", s, i), remote(src, dst, x_s.at[s, i], x_r.at[s, i], peer))
@@ -221,7 +221,7 @@
         x_copy(s, 4, own, xb.at[s, 1, 0], other)
         square = jnp.concatenate(squares, axis=0)
         flat = jnp.sum(jnp.where(diagonal, square, 0.0), axis=0, keepdims=True)
-        mt[s, 0] = jnp.broadcast_to(flat, mt.shape[2:])
+        mt[s, 0] = flat
         for cs, xr in mates:
             there = cs * XN + (XN - xr) % XN
             remote(mt.at[s, 0], mt.at[s, there], m_s.at[s], m_r.at[s], near(cs, xr)).start()
@@ -249,7 +249,7 @@
             acts = acts + jnp.dot(xb[s, 0, xr], wgu[xr], preferred_element_type=F32)
         receive("m", s)
         total = sum(mt[s, r] for r in range(CN * XN))
-        inv = lax.rsqrt(total[0:1] / depth + 1e-06)
+        inv = lax.rsqrt(total / depth + 1e-06)
         inv = jnp.sum(jnp.where(diagonal, inv, 0.0), axis=1, keepdims=True)
         for i, xr in ((4, 0), (7, XN - 1), (8, 1), (9, 2)):
             receive("x", s, i)
@@ -383,7 +383,7 @@
             blocks,
             blocks,
             pltpu.VMEM((stages, CN, XN, slots, chan), BF),
-            pltpu.VMEM((stages, mates, 8, slots), F32),
+            pltpu.VMEM((stages, mates, 1, slots), F32),
             pltpu.VMEM((stages, CN, XN, slots, hid), BF),
             blocks,
             blocks,

time: 79.4 us -> 79.5 us (level)
  no operation moved by 1% of the time
where the time goes in v3:
time: 79.5 us; the launch traced here: 79.3 us
  Pallas kernels  77.9 us (98%)
  local copies, waits for them, and re-layouts  1.47 us (2%)
    pallas_call x1, Pallas kernels, per_device(): pl.pallas_call(kernel, out_shape=jax.ShapeDtypeStruct(tokens.shape, token...  77.9 us

profile of v3, /device:TPU:1, one launch (start us, length us, event | category | flops | bytes accessed | tf_op | source)
XLA Modules:
  0.0 79.3 jit_solution(17086446011880176208)
XLA Ops:
  0.0 77.9 %routed_experts.1 = bf16[2,32,512]{2,1,0:T(8,128)(2,1)} custom-call(bf16[2,32,512]{2,1,0:T(8,128)(2,1)} %tok_in.1, bf16[512]{0:T(512)(128)(2,1)} %gain.1, bf16[64,512]{1,0:T(8,128)(2,1)} %bitcast.2, s32[2,4,32]{2,1,0:T(4,128)} %bitcast.3, bf16[1,4096,128]{2,1,0:T(8,128)(2,1)} %wg.1, bf16[1,4096,128]{2,1,0:T(8,128)(2,1)} %wu.1, bf16[1,1024,512]{2,1,0:T(8,128)(2,1)} %wd.1), custom_call_target="tpu_custom_call" | custom-call | tf_op jit(solution)/shard_map/routed_experts/pallas_call | solution.py:369
  77.9 1.5 %copy.9 = bf16[2,32,512]{2,1,0:T(8,128)(2,1)} copy(bf16[2,32,512]{2,1,0:T(8,128)(2,1)} %routed_experts.1) | data formatting | bytes 131072
